TPU v7x, 256 devices: a whole 4x4x8 slice. The times are simulated.
256 devices in a mesh: fsdp: 32 (over x, z_lo, core), tp: 8 (over y, z_hi).
Axes of the slice: x: 4, y: 4, z: 8 (z_hi: 2, z_lo: 4; z = z_hi * 4 + z_lo), core: 2. Of those that a mesh axis runs over, the one named last changes fastest.
Arguments:
- hidden_in: bfloat16 [32768, 5120], P('fsdp', 'tp'), may hold values from -6 to 6
- out_grad: bfloat16 [32768, 5120], P('fsdp', 'tp'), may hold values from -36 to 36
- rewards: float32 [64], P('fsdp'), may hold values from -5 to 5
- group_ids: int32 [64], replicated, may hold values from 0 to 7, as said below
- weight: bfloat16 [5120, 5120], P('fsdp', 'tp'), may hold values from -0.078125 to 0.078125
- adam_m: float32 [5120, 5120], P('fsdp', 'tp'), may hold values from -6 to 6
- adam_v: float32 [5120, 5120], P('fsdp', 'tp'), may hold values from 0.05 to 2
- given_queries: bfloat16 [512, 4, 5120], P('fsdp', None, 'tp'), may hold values from -24 to 24
- given_keys: bfloat16 [512, 4, 1024], P('fsdp', None, 'tp'), may hold values from -4 to 4
- given_values: bfloat16 [512, 4, 1024], P('fsdp', None, 'tp'), may hold values from -12 to 12
- stored_keys: bfloat16 [512, 8, 512, 128], P('fsdp', 'tp'), may hold values from -24 to 24
- stored_values: bfloat16 [512, 8, 512, 128], P('fsdp', 'tp'), may hold values from -12 to 12
- cache_fill_length: int32 [512], P('fsdp'), may hold values from 128 to 508
Outputs:
- new_weight: bfloat16 [5120, 5120], P('fsdp', 'tp')
- new_m: float32 [5120, 5120], P('fsdp', 'tp')
- new_v: float32 [5120, 5120], P('fsdp', 'tp')
- layer_out: float32 [512, 4, 5120], P('fsdp', None, 'tp')
Inputs may be any that keep to these rules, and one draw needn't show every extreme that they name: `group_ids`: each group number names exactly 8 sequences.
All inputs are finite; a program needn't handle non-finite values.
Results may differ from a plain program's by a relative error of at most 0.0059.
Values may be sent and summed in bfloat16 or wider, within the bound.
No kernel may reach another device: no remote copies, remote signals or barrier semaphores. Data moves between devices by JAX's collectives and lax.ppermute only.
A program may use at most 128 MiB of HBM per device.

v0:
```python
import math

import jax
import jax.numpy as jnp
from jax import lax
from jax.sharding import PartitionSpec as P

GSIZE = 8
OPT_STEP = 10


beta_one = 0.9
beta_two = 0.95
adam_eps = 1e-08
learn_rate = 0.002
decay_rate = 0.1
std_floor = 0.75


def attend_local(query_in, key_new, value_new, key_cache, value_cache, lengths):
    row_count = query_in.shape[0]
    step_count = query_in.shape[1]
    kv_heads = key_cache.shape[1]
    cache_size = key_cache.shape[2]
    head_dim = key_cache.shape[3]
    group_size = query_in.shape[2] // (kv_heads * head_dim)
    scaling = 1.0 / math.sqrt(head_dim)
    query_heads = query_in.reshape(row_count, step_count, kv_heads, group_size, head_dim)
    fresh_keys = key_new.reshape(row_count, step_count, kv_heads, head_dim)
    fresh_values = value_new.reshape(row_count, step_count, kv_heads, head_dim)
    cache_score = (
        jnp.einsum("rsKgd,rKcd->rKgsc", query_heads, key_cache, preferred_element_type=jnp.float32)
        * scaling
    )
    fresh_score = (
        jnp.einsum("rsKgd,rtKd->rKgst", query_heads, fresh_keys, preferred_element_type=jnp.float32)
        * scaling
    )
    cache_mask = jnp.arange(cache_size, dtype=jnp.int32)[None, :] < lengths[:, None]
    step_index = jnp.arange(step_count, dtype=jnp.int32)
    fresh_mask = step_index[None, :] <= step_index[:, None]
    cache_score = jnp.where(cache_mask[:, None, None, None, :], cache_score, -jnp.inf)
    fresh_score = jnp.where(fresh_mask, fresh_score, -jnp.inf)
    peak_score = jnp.maximum(
        jnp.max(cache_score, axis=-1, keepdims=True), jnp.max(fresh_score, axis=-1, keepdims=True)
    )
    cache_exp = jnp.exp(cache_score - peak_score)
    fresh_exp = jnp.exp(fresh_score - peak_score)
    total_exp = jnp.sum(cache_exp, axis=-1, keepdims=True) + jnp.sum(
        fresh_exp, axis=-1, keepdims=True
    )
    cache_prob = (cache_exp / total_exp).astype(jnp.bfloat16)
    fresh_prob = (fresh_exp / total_exp).astype(jnp.bfloat16)
    mixed = jnp.einsum(
        "rKgsc,rKcd->rsKgd", cache_prob, value_cache, preferred_element_type=jnp.float32
    )
    mixed = mixed + jnp.einsum(
        "rKgst,rtKd->rsKgd", fresh_prob, fresh_values, preferred_element_type=jnp.float32
    )
    return mixed.reshape(row_count, step_count, kv_heads * group_size * head_dim).astype(
        jnp.bfloat16
    )


def per_device(
    hidden_in,
    out_grad,
    rewards,
    group_ids,
    weight,
    adam_m,
    adam_v,
    given_queries,
    given_keys,
    given_values,
    stored_keys,
    stored_values,
    cache_fill_length,
):
    seq_dev = rewards.shape[0]
    seq_total = seq_dev * lax.axis_size("fsdp")
    group_count = seq_total // GSIZE
    position = lax.axis_index("fsdp")
    local_ids = lax.dynamic_slice_in_dim(group_ids, position * seq_dev, seq_dev)
    labels = jnp.arange(group_count, dtype=jnp.int32)
    local_member = (local_ids[:, None] == labels[None, :]).astype(jnp.float32)
    every_reward = lax.all_gather(rewards, "fsdp", axis=0, tiled=True)
    member = (group_ids[:, None] == labels[None, :]).astype(jnp.float32)
    group_mean = jnp.sum(member * every_reward[:, None], axis=0) / GSIZE
    spread_all = every_reward - jnp.sum(member * group_mean[None, :], axis=1)
    group_var = jnp.sum(member * (spread_all * spread_all)[:, None], axis=0) / (GSIZE - 1)
    own_mean = jnp.sum(local_member * group_mean[None, :], axis=1)
    own_std = jnp.sqrt(jnp.sum(local_member * group_var[None, :], axis=1))
    advantage = (rewards - own_mean) / jnp.maximum(own_std, std_floor)
    token_count = hidden_in.shape[0]
    token_adv = jnp.repeat(advantage, token_count // seq_dev)
    weighted = (hidden_in.astype(jnp.float32) * token_adv[:, None] / seq_total).astype(jnp.bfloat16)
    full_grad = lax.all_gather(out_grad, "tp", axis=1, tiled=True)
    gradient = lax.psum_scatter(
        lax.dot_general(
            full_grad, weighted, (((0,), (0,)), ((), ())), preferred_element_type=jnp.float32
        ),
        "fsdp",
        scatter_dimension=0,
        tiled=True,
    )
    new_m = beta_one * adam_m + (1.0 - beta_one) * gradient
    new_v = beta_two * adam_v + (1.0 - beta_two) * gradient * gradient
    correct_one = 1.0 - beta_one**OPT_STEP
    correct_two = 1.0 - beta_two**OPT_STEP
    update = new_m / correct_one / (jnp.sqrt(new_v / correct_two) + adam_eps)
    new_weight = (
        weight.astype(jnp.float32) * (1.0 - learn_rate * decay_rate) - learn_rate * update
    ).astype(jnp.bfloat16)
    attn = attend_local(
        given_queries, given_keys, given_values, stored_keys, stored_values, cache_fill_length
    )
    row_count = attn.shape[0]
    step_count = attn.shape[1]
    attn_flat = attn.reshape(row_count * step_count, attn.shape[2])
    partial_out = lax.dot_general(
        attn_flat,
        lax.all_gather(new_weight, "fsdp", axis=0, tiled=True),
        (((1,), (1,)), ((), ())),
        preferred_element_type=jnp.float32,
    )
    summed = lax.psum_scatter(partial_out, "tp", scatter_dimension=1, tiled=True)
    layer_out = summed.reshape(row_count, step_count, summed.shape[1])
    return (new_weight, new_m, new_v, layer_out)


def solution(mesh):
    in_specs = (
        P("fsdp", "tp"),
        P("fsdp", "tp"),
        P("fsdp"),
        P(),
        P("fsdp", "tp"),
        P("fsdp", "tp"),
        P("fsdp", "tp"),
        P("fsdp", None, "tp"),
        P("fsdp", None, "tp"),
        P("fsdp", None, "tp"),
        P("fsdp", "tp", None, None),
        P("fsdp", "tp", None, None),
        P("fsdp"),
    )
    out_specs = (P("fsdp", "tp"), P("fsdp", "tp"), P("fsdp", "tp"), P("fsdp", None, "tp"))
    return jax.shard_map(
        per_device, mesh=mesh, in_specs=in_specs, out_specs=out_specs, check_vma=False
    )
```

profile of v0, /device:TPU:102, one launch (start us, length us, event | category | flops | bytes accessed | tf_op | source)
XLA Modules:
  0.0 582.6 jit_solution(10707722443062286807)
XLA Ops:
  7.2 0.0 copy-start
  7.2 0.0 all-gather.3.cloned.1.call-start
  7.2 0.7 all-gather.3.cloned.1.call-update
  7.9 0.0 reduce-scatter.7.cloned.1.call-start
  8.0 1.3 dynamic-slice
  9.9 0.7 dynamic_slice.3
  10.6 0.8 dynamic-update-slice
  11.5 67.0 %all-reduce = f32[64]{0:T(128)S(1)} all-reduce(f32[64]{0:T(128)S(1)} %dynamic-update-slice), channel_id=1, replica_groups=mesh['fsdp'=32,'tp'=8] {'fsdp'}, use_global_device_ids=true, to_apply=%add | all-reduce | flops 64 | bytes 512
  78.5 0.8 select_reduce_fusion.2
  79.3 0.8 select_reduce_fusion.1
  80.0 0.8 select_reduce_fusion
  80.8 0.2 select_reduce_fusion.4
  81.0 0.7 maximum_divide_fusion
  81.7 0.1 broadcast_bitcast_fusion
  81.8 124.2 %all-gather.3.cloned.1.call-done = bf16[1024,5120]{1,0:T(8,128)(2,1)} async-done(((bf16[1024,640]{1,0:T(8,128)(2,1)}), bf16[1024,5120]{1,0:T(8,128)(2,1)}) %all-gather.3.cloned.1.call-update) | async-done | bytes 10485776 | tf_op jit(solution)/shard_map/all_gather | solution.py:98
  206.0 13.0 %convolution_bitcast_fusion = f32[5120,640]{0,1:T(8,128)} fusion(bf16[1024,5120]{1,0:T(8,128)(2,1)} %all-gather.3.cloned.1.call-done, bf16[1024,640]{1,0:T(8,128)(2,1)} %param.13, f32[1024]{0:T(1024)S(1)} %bitcast.80), kind=kOutput, calls=%fused_computation | convolution fusion | flops 6713507840 | bytes 24907776 | tf_op jit(solution)/shard_map/dot_general | solution.py:100
  219.0 14.0 %copy.62 = f32[5120,640]{1,0:T(8,128)} copy(f32[5120,640]{0,1:T(8,128)} %convolution_bitcast_fusion) | data formatting | bytes 26214400
  233.0 0.0 reduce-scatter.7.cloned.1.call-update
  233.0 0.0 copy-start.4
  233.0 0.0 copy-start.5
  233.0 0.0 copy-start.7
  233.0 0.0 all-gather.5.cloned.1.call-start
  233.1 177.5 %reduce-scatter.7.cloned.1.call-done = f32[160,640]{1,0:T(8,128)} async-done(((f32[5120,640]{1,0:T(8,128)}), f32[160,640]{1,0:T(8,128)}) %reduce-scatter.7.cloned.1.call-update) | async-done | bytes 409616 | tf_op jit(solution)/shard_map/reduce_scatter | solution.py:99
  410.6 0.0 copy-done.1
  410.6 0.0 copy-done.2
  410.6 0.0 copy-done.3
  410.6 2.2 subtract_convert_fusion
  412.7 0.0 all-gather.5.cloned.1.call-update
  412.8 0.0 reduce-scatter.5.cloned.1.call-start
  412.8 0.0 copy-done.4
  412.9 0.0 copy-start.8
  412.9 0.0 copy-done.5
  412.9 0.1 iota_compare_fusion
  413.0 0.0 copy-done.7
  413.0 0.7 fusion.42
  413.7 0.0 copy-done
  413.7 0.0 copy-start.6
  413.7 0.9 fusion.41
  414.6 0.1 fusion.30
  414.8 0.4 fusion.26
  415.2 0.3 fusion.34
  415.4 0.0 copy-done.6
  415.4 0.6 fusion.21
  416.1 64.1 %all-gather.5.cloned.1.call-done = bf16[5120,640]{1,0:T(8,128)(2,1)} async-done(((bf16[160,640]{1,0:T(8,128)(2,1)}), bf16[5120,640]{1,0:T(8,128)(2,1)}) %all-gather.5.cloned.1.call-update) | async-done | bytes 6553616 | tf_op jit(solution)/shard_map/all_gather | solution.py:123
  480.1 6.0 %fusion.31 = f32[64,5120]{1,0:T(8,128)} fusion(bf16[5120,640]{1,0:T(8,128)(2,1)} %all-gather.5.cloned.1.call-done, bf16[8,8,5,128]{3,2,1,0:T(8,128)(2,1)S(1)} %bitcast.81), kind=kOutput, calls=%fused_computation.29 | convolution fusion | flops 419430400 | bytes 7946240 | tf_op jit(solution)/shard_map/dot_general | solution.py:121
  486.2 0.0 reduce-scatter.5.cloned.1.call-update
  486.2 88.2 %reduce-scatter.5.cloned.1.call-done = f32[64,640]{1,0:T(8,128)} async-done(((f32[64,5120]{1,0:T(8,128)}), f32[64,640]{1,0:T(8,128)}) %reduce-scatter.5.cloned.1.call-update) | async-done | bytes 163856 | tf_op jit(solution)/shard_map/reduce_scatter | solution.py:127
  574.4 1.6 reshape.117
  (13 shorter events, 0.1 us)
Async XLA Ops:
  7.2 406.5 %copy-start = (bf16[16,1,512,128]{3,2,1,0:T(8,128)(2,1)S(1)}, bf16[16,1,512,128]{3,2,1,0:T(8,128)(2,1)}, u32[]{:S(2)}) copy-start(bf16[16,1,512,128]{3,2,1,0:T(8,128)(2,1)} %param.23) | copy-start | bytes 6291460
  7.2 198.8 %all-gather.3.cloned.1.call-start = ((), (), s32[]{:S(2)}) async-start(), calls=%async_computation.2 | async-start | bytes 11796480 | tf_op jit(solution)/shard_map/all_gather | solution.py:98
  7.9 402.7 %reduce-scatter.7.cloned.1.call-start = ((), (), s32[]{:S(2)}) async-start(), calls=%async_computation.5 | async-start | bytes 13516800 | tf_op jit(solution)/shard_map/reduce_scatter | solution.py:99
  233.0 177.6 %copy-start.1 = (f32[160,640]{1,0:T(8,128)S(1)}, f32[160,640]{1,0:T(8,128)}, u32[]{:S(2)}) copy-start(f32[160,640]{1,0:T(8,128)} %param.18) | copy-start | bytes 1228804
  233.0 177.6 %copy-start.2 = (f32[160,640]{1,0:T(8,128)S(1)}, f32[160,640]{1,0:T(8,128)}, u32[]{:S(2)}) copy-start(f32[160,640]{1,0:T(8,128)} %param.19) | copy-start | bytes 1228804
  233.0 177.6 %copy-start.3 = (bf16[160,640]{1,0:T(8,128)(2,1)S(1)}, bf16[160,640]{1,0:T(8,128)(2,1)}, u32[]{:S(2)}) copy-start(bf16[160,640]{1,0:T(8,128)(2,1)} %param.17) | copy-start | bytes 614404
  233.0 179.8 %copy-start.4 = (bf16[16,4,640]{2,1,0:T(4,128)(2,1)S(1)}, bf16[16,4,640]{2,1,0:T(4,128)(2,1)}, u32[]{:S(2)}) copy-start(bf16[16,4,640]{2,1,0:T(4,128)(2,1)} %param.20) | copy-start | bytes 245764
  233.0 179.9 %copy-start.5 = (s32[16]{0:T(128)S(1)}, s32[16]{0:T(128)}, u32[]{:S(2)}) copy-start(s32[16]{0:T(128)} %param.25) | copy-start | bytes 196
  233.0 180.0 %copy-start.7 = (bf16[16,4,128]{2,1,0:T(4,128)(2,1)S(1)}, bf16[16,4,128]{2,1,0:T(4,128)(2,1)}, u32[]{:S(2)}) copy-start(bf16[16,4,128]{2,1,0:T(4,128)(2,1)} %param.21) | copy-start | bytes 49156
  233.0 247.1 %all-gather.5.cloned.1.call-start = ((), (), s32[]{:S(2)}) async-start(), calls=%async_computation.3 | async-start | bytes 6758400 | tf_op jit(solution)/shard_map/all_gather | solution.py:123
  412.8 161.7 %reduce-scatter.5.cloned.1.call-start = ((), (), s32[]{:S(2)}) async-start(), calls=%async_computation.4 | async-start | bytes 1474560 | tf_op jit(solution)/shard_map/reduce_scatter | solution.py:127
  412.9 2.3 copy-start.8
  413.7 1.7 copy-start.6
Sparse Core Ops, SparseCore 0:
  10.6 195.3 all-gather.2
  233.1 177.4 reduce-scatter.6
  413.2 66.9 all-gather.4
  486.3 88.0 reduce-scatter.4
where the time goes:
time: 587 us; the launch traced here: 583 us
  waiting for transfers between devices  455 us (78%)
  blocking collectives  67 us (11%)
  matrix products  21.5 us (4%)
  local copies, waits for them, and re-layouts  18.6 us (3%)
  between operations  14.6 us (2%)
  other arithmetic  5.95 us (1%)
    reduce_scatter x1, waiting for transfers between devices, per_device(): lax.psum_scatter(lax.dot_general(full_grad, weighted, (((0,), (0,)), ((),...  178 us
    all_gather x1, waiting for transfers between devices, per_device(): full_grad = lax.all_gather(out_grad, 'tp', axis=1, tiled=True)  124 us
    reduce_scatter x1, waiting for transfers between devices, per_device(): lax.psum_scatter(partial_out, 'tp', scatter_dimension=1, tiled=True)  88.2 us
    unnamed x1, blocking collectives  67 us
    all_gather x1, waiting for transfers between devices, per_device(): lax.all_gather(new_weight, 'fsdp', axis=0, tiled=True)  64.1 us
    unnamed x24, local copies, waits for them, and re-layouts  16.2 us
    dot_general x1, matrix products, per_device(): lax.dot_general(full_grad, weighted, (((0,), (0,)), ((), ())), preferred_...  13 us
  transfers between devices with their start and end apart: 4, of which 4 were waited for; matrix products, arithmetic and copies ran while one was open for 2% of the time, Pallas kernels for 0%

commit v1 on v0

--- a/solution.py
+++ b/solution.py
@@ -7,7 +7,6 @@
 
 GSIZE = 8
 OPT_STEP = 10
-
 
 beta_one = 0.9
 beta_two = 0.95
@@ -15,6 +14,28 @@
 learn_rate = 0.002
 decay_rate = 0.1
 std_floor = 0.75
+
+NX, ZL, CORES, NY, ZH = 4, 4, 2, 4, 2
+
+
+def send(value, dest):
+    pairs = []
+    for x in range(NX):
+        for zl in range(ZL):
+            for c in range(CORES):
+                for y in range(NY):
+                    for zh in range(ZH):
+                        to = dest(x, zl, c, y, zh)
+                        pairs.append((flat(x, zl, c, y, zh), flat(*to)))
+    return lax.ppermute(value, ("fsdp", "tp"), pairs)
+
+
+def flat(x, zl, c, y, zh):
+    return ((x * ZL + zl) * CORES + c) * (NY * ZH) + y * ZH + zh
+
+
+def other_core(value):
+    return send(value, lambda x, zl, c, y, zh: (x, zl, 1 - c, y, zh))
 
 
 def attend_local(query_in, key_new, value_new, key_cache, value_cache, lengths):
@@ -60,6 +81,25 @@
     return mixed.reshape(row_count, step_count, kv_heads * group_size * head_dim).astype(
         jnp.bfloat16
     )
+
+
+def chip_advantage(rewards, group_ids, position, core):
+    seq_dev = rewards.shape[0]
+    devices = lax.axis_size("fsdp")
+    group_count = seq_dev * devices // GSIZE
+    tile = jnp.zeros((8, 128), jnp.float32).at[0, :seq_dev].set(rewards)
+    tiles = lax.all_gather(tile, "fsdp", axis=0)
+    every_reward = tiles[:, 0, :seq_dev].reshape(-1)
+    labels = jnp.arange(group_count, dtype=jnp.int32)
+    member = (group_ids[:, None] == labels[None, :]).astype(jnp.float32)
+    group_mean = jnp.sum(member * every_reward[:, None], axis=0) / GSIZE
+    spread = every_reward - jnp.sum(member * group_mean[None, :], axis=1)
+    group_var = jnp.sum(member * (spread * spread)[:, None], axis=0) / (GSIZE - 1)
+    own_std = jnp.sqrt(jnp.sum(member * group_var[None, :], axis=1))
+    advantage = spread / jnp.maximum(own_std, std_floor)
+    mine = lax.dynamic_slice_in_dim(advantage, position * seq_dev, seq_dev)
+    theirs = lax.dynamic_slice_in_dim(advantage, (position + 1 - 2 * core) * seq_dev, seq_dev)
+    return mine, theirs
 
 
 def per_device(
@@ -77,33 +117,73 @@
     stored_values,
     cache_fill_length,
 ):
-    seq_dev = rewards.shape[0]
-    seq_total = seq_dev * lax.axis_size("fsdp")
-    group_count = seq_total // GSIZE
     position = lax.axis_index("fsdp")
-    local_ids = lax.dynamic_slice_in_dim(group_ids, position * seq_dev, seq_dev)
-    labels = jnp.arange(group_count, dtype=jnp.int32)
-    local_member = (local_ids[:, None] == labels[None, :]).astype(jnp.float32)
-    every_reward = lax.all_gather(rewards, "fsdp", axis=0, tiled=True)
-    member = (group_ids[:, None] == labels[None, :]).astype(jnp.float32)
-    group_mean = jnp.sum(member * every_reward[:, None], axis=0) / GSIZE
-    spread_all = every_reward - jnp.sum(member * group_mean[None, :], axis=1)
-    group_var = jnp.sum(member * (spread_all * spread_all)[:, None], axis=0) / (GSIZE - 1)
-    own_mean = jnp.sum(local_member * group_mean[None, :], axis=1)
-    own_std = jnp.sqrt(jnp.sum(local_member * group_var[None, :], axis=1))
-    advantage = (rewards - own_mean) / jnp.maximum(own_std, std_floor)
-    token_count = hidden_in.shape[0]
-    token_adv = jnp.repeat(advantage, token_count // seq_dev)
-    weighted = (hidden_in.astype(jnp.float32) * token_adv[:, None] / seq_total).astype(jnp.bfloat16)
-    full_grad = lax.all_gather(out_grad, "tp", axis=1, tiled=True)
-    gradient = lax.psum_scatter(
-        lax.dot_general(
-            full_grad, weighted, (((0,), (0,)), ((), ())), preferred_element_type=jnp.float32
-        ),
-        "fsdp",
-        scatter_dimension=0,
-        tiled=True,
-    )
+    tp_at = lax.axis_index("tp")
+    x, zl, core = position // (ZL * CORES), (position // CORES) % ZL, position % CORES
+    y, zh = tp_at // ZH, tp_at % ZH
+    tokens, width = hidden_in.shape
+    rows = weight.shape[0]
+    seqs = rewards.shape[0] * lax.axis_size("fsdp")
+
+    hidden_far = send(hidden_in, lambda x, zl, c, y, zh: (x, zl, c, y, 1 - zh))
+
+    parts = out_grad.reshape(tokens, 2, CORES, rows)
+    even, odd = parts[:, :, 0], parts[:, :, 1]
+    keep = jnp.where(core == 0, even, odd).reshape(tokens, 2 * rows)
+    give = jnp.where(core == 0, odd, even).reshape(tokens, 2 * rows)
+    grad_near = jnp.concatenate([keep, other_core(give)], axis=0)
+    grads = [grad_near] + [
+        send(grad_near, lambda x, zl, c, y, zh, d=d: (x, zl, c, (y - d) % NY, zh)) for d in (1, 2, 3)
+    ]
+
+    attn = attend_local(
+        given_queries, given_keys, given_values, stored_keys, stored_values, cache_fill_length
+    )
+    row_count, step_count = attn.shape[0], attn.shape[1]
+    every_attn = lax.all_gather(
+        attn.reshape(row_count * step_count, width), "fsdp", axis=0, tiled=True
+    )
+
+    mine, theirs = chip_advantage(rewards, group_ids, position, core)
+    scale = jnp.repeat(jnp.concatenate([mine, theirs]), tokens // rewards.shape[0])[:, None]
+
+    def weighted(hidden):
+        both = jnp.concatenate([hidden, other_core(hidden)], axis=0)
+        return (both.astype(jnp.float32) * scale / seqs).astype(jnp.bfloat16)
+
+    halves = []
+    for hidden in (hidden_in, hidden_far):
+        factor = weighted(hidden)
+        tiles = jnp.stack(
+            [
+                lax.dot_general(
+                    g, factor, (((0,), (0,)), ((), ())), preferred_element_type=jnp.float32
+                ).astype(jnp.bfloat16)
+                for g in grads
+            ]
+        )
+        total = None
+        for s in range(NX):
+            tile = lax.dynamic_index_in_dim(tiles, (x + s - y) % NX, 0, keepdims=False)
+            if s:
+                tile = send(tile, lambda x, zl, c, y, zh, s=s: ((x + s) % NX, zl, c, y, zh))
+            tile = tile.astype(jnp.float32)
+            total = tile if total is None else total + tile
+        halves.append(total.astype(jnp.bfloat16).reshape(2, rows, width))
+
+    near, far = halves
+    blocks = jnp.concatenate(
+        [jnp.where(zh == 0, near, far), jnp.where(zh == 0, far, near)], axis=0
+    )
+    gradient = None
+    for s in range(4):
+        block = lax.dynamic_index_in_dim(blocks, zl ^ s, 0, keepdims=False)
+        block = send(
+            block,
+            lambda x, zl, c, y, zh, s=s: (x, 2 * zh + ((zl ^ s) & 1), c, y, (zl ^ s) >> 1),
+        ).astype(jnp.float32)
+        gradient = block if gradient is None else gradient + block
+
     new_m = beta_one * adam_m + (1.0 - beta_one) * gradient
     new_v = beta_two * adam_v + (1.0 - beta_two) * gradient * gradient
     correct_one = 1.0 - beta_one**OPT_STEP
@@ -112,20 +192,34 @@
     new_weight = (
         weight.astype(jnp.float32) * (1.0 - learn_rate * decay_rate) - learn_rate * update
     ).astype(jnp.bfloat16)
-    attn = attend_local(
-        given_queries, given_keys, given_values, stored_keys, stored_values, cache_fill_length
-    )
-    row_count = attn.shape[0]
-    step_count = attn.shape[1]
-    attn_flat = attn.reshape(row_count * step_count, attn.shape[2])
+
     partial_out = lax.dot_general(
-        attn_flat,
-        lax.all_gather(new_weight, "fsdp", axis=0, tiled=True),
-        (((1,), (1,)), ((), ())),
-        preferred_element_type=jnp.float32,
-    )
-    summed = lax.psum_scatter(partial_out, "tp", scatter_dimension=1, tiled=True)
-    layer_out = summed.reshape(row_count, step_count, summed.shape[1])
+        every_attn, new_weight, (((1,), (1,)), ((), ())), preferred_element_type=jnp.float32
+    ).astype(jnp.bfloat16)
+    partial_out = partial_out.reshape(NY, -1, rows)
+    summed = None
+    for s in range(NY):
+        block = lax.dynamic_index_in_dim(partial_out, y ^ s, 0, keepdims=False)
+        block = send(block, lambda x, zl, c, y, zh, s=s: (y ^ s, zl, c, x, zh)).astype(jnp.float32)
+        summed = block if summed is None else summed + block
+    summed = summed.reshape(ZH, -1, rows)
+    keep = lax.dynamic_index_in_dim(summed, zh, 0, keepdims=False)
+    give = lax.dynamic_index_in_dim(summed, 1 - zh, 0, keepdims=False)
+    summed = keep + send(give, lambda x, zl, c, y, zh: (x, zl, c, y, 1 - zh))
+    summed = summed.reshape(4, -1, rows)
+    place = (zl % 2) * CORES + core
+    got = []
+    for s in range(4):
+        block = lax.dynamic_index_in_dim(summed, place ^ s, 0, keepdims=False)
+
+        def dest(x, zl, c, y, zh, s=s):
+            at = ((zl % 2) * CORES + c) ^ s
+            return (x, 2 * zh + at // CORES, at % CORES, y, zl // 2)
+
+        got.append(send(block, dest))
+    got = jnp.stack(got)
+    columns = [lax.dynamic_index_in_dim(got, place ^ j, 0, keepdims=False) for j in range(4)]
+    layer_out = jnp.concatenate(columns, axis=1).reshape(row_count, step_count, width)
     return (new_weight, new_m, new_v, layer_out)
 
 

time: 587 us -> 312 us (0.53)
  waiting for transfers between devices: 455 us -> 110 us
  starting transfers between devices: 0.16 us -> 50.8 us
  blocking collectives: 67 us -> 86.2 us
  local copies, waits for them, and re-layouts: 18.6 us -> 9.39 us
  matrix products: 21.5 us -> 29.4 us
    reduce_scatter x2 -> x0, waiting for transfers between devices: 266 us -> none  [the longest x1 178 us: per_device(): lax.psum_scatter(lax.dot_general(full_grad, weighted, (((0,), (0,)), ((),...]
    all_gather x2 -> x1, waiting for transfers between devices: 188 us -> 0.01 us  [per_device(): lax.all_gather(attn.reshape(row_count * step_count, width), 'fsdp', axis=...]
    ppermute x0 -> x26, waiting for transfers between devices: none -> 110 us  [send(): return lax.ppermute(value, ('fsdp', 'tp'), pairs)]
    all_gather x0 -> x1, blocking collectives: none -> 86.2 us  [chip_advantage(): tiles = lax.all_gather(tile, 'fsdp', axis=0)]
    unnamed x1 -> x0, blocking collectives: 67 us -> none
    ppermute x0 -> x26, starting transfers between devices: none -> 50.8 us  [send(): return lax.ppermute(value, ('fsdp', 'tp'), pairs)]
    unnamed x24 -> x41, local copies, waits for them, and re-layouts: 16.2 us -> 4.41 us
    dot_general x2 -> x9, matrix products: 19 us -> 27 us  [the longest x8 24.2 us: per_device(): lax.dot_general(g, factor, (((0,), (0,)), ((), ())), preferred_element_ty...]
  transfers between devices with their start and end apart: 4 -> 27, of which waited for: 4 -> 15; matrix products, arithmetic and copies ran while one was open for 2% -> 13% of each run, Pallas kernels for 0% -> 0%
where the time goes in v1:
time: 312 us
  waiting for transfers between devices  110 us (35%)
  blocking collectives  86.2 us (28%)
  starting transfers between devices  50.8 us (16%)
  matrix products  29.4 us (9%)
  between operations  14.6 us (5%)
  other arithmetic  10.7 us (3%)
  local copies, waits for them, and re-layouts  9.39 us (3%)
    ppermute x26, waiting for transfers between devices, send(): return lax.ppermute(value, ('fsdp', 'tp'), pairs)  110 us
    all_gather x1, blocking collectives, chip_advantage(): tiles = lax.all_gather(tile, 'fsdp', axis=0)  86.2 us
    ppermute x26, starting transfers between devices, send(): return lax.ppermute(value, ('fsdp', 'tp'), pairs)  50.8 us
    dot_general x8, matrix products, per_device(): lax.dot_general(g, factor, (((0,), (0,)), ((), ())), preferred_element_ty...  24.2 us
  transfers between devices with their start and end apart: 27, of which 15 were waited for; matrix products, arithmetic and copies ran while one was open for 13% of the time, Pallas kernels for 0%

profile of v1, /device:TPU:102, one launch (start us, length us, event | category | flops | bytes accessed | tf_op | source)
XLA Modules:
  0.0 311.6 jit_solution(1351904603972353989)
XLA Ops:
  7.2 4.6 %collective-permute-start.8 = (bf16[1024,640]{1,0:T(8,128)(2,1)}, bf16[1024,640]{1,0:T(8,128)(2,1)}, u32[]{:S(2)}, u32[]{:S(2)}) collective-permute-start(bf16[1024,640]{1,0:T(8,128)(2,1)} %param.15), channel_id=1, source_target_pairs={{0,1},{1,0},{2,3},{3,2},{4,5},{5,4},{6,7},{7,6},{8,9},{9,8},{10,11... | collective-permute-start | bytes 3932168 | tf_op jit(solution)/shard_map/ppermute | solution.py:30
  11.8 1.6 copy.49
  13.5 1.2 broadcast_select_fusion.1
  19.1 86.2 %all_gather.10 = f32[32,8,128]{2,1,0:T(8,128)S(1)} all-gather(f32[1,8,128]{2,1,0:T(8,128)S(1)} %scatter.4), channel_id=1, replica_groups=mesh['fsdp'=32,'tp'=8] {'fsdp'}, dimensions={0}, use_global_device_ids=true | all-gather | bytes 135168 | tf_op jit(solution)/shard_map/all_gather | solution.py:91
  105.8 1.2 pad_maximum_fusion.2
  107.0 1.6 collective-permute-start.4
  108.6 2.9 collective-permute-start.3
  111.7 1.4 collective-permute-start.2
  113.4 3.1 %fusion.16 = bf16[1,320,640]{2,1,0:T(8,128)(2,1)S(1)} fusion(bf16[1024,320]{0,1:T(8,128)(2,1)S(1)} %collective-permute-done, bf16[1024,320]{0,1:T(8,128)(2,1)S(1)} %bitcast.170, bf16[1024,640]{1,0:T(8,128)(2,1)} %collective-permute-done.1, bf16[1024,640]{1,0:T(8,128)(2,1)} %param.15, f32[2048]{0:T(1024)S(1)} %bitcast.186), kind=kOutput, calls=%fused_computation.22 | convolution fusion | flops 850862080 | bytes 4349952 | tf_op jit(solution)/shard_map/dot_general | solution.py:159
  116.5 23.0 %collective-permute-done.4 = bf16[2048,320]{0,1:T(8,128)(2,1)} collective-permute-done((bf16[2048,320]{0,1:T(8,128)(2,1)}, bf16[2048,320]{0,1:T(8,128)(2,1)}, u32[]{:S(2)}, u32[]{:S(2)}) %collective-permute-start.4) | collective-permute-done | bytes 1310752 | tf_op jit(solution)/shard_map/ppermute | solution.py:30
  139.6 3.1 fusion.19
  142.7 26.2 %collective-permute-done.3 = bf16[2048,320]{0,1:T(8,128)(2,1)} collective-permute-done((bf16[2048,320]{0,1:T(8,128)(2,1)}, bf16[2048,320]{0,1:T(8,128)(2,1)}, u32[]{:S(2)}, u32[]{:S(2)}) %collective-permute-start.3) | collective-permute-done | bytes 1310752 | tf_op jit(solution)/shard_map/ppermute | solution.py:30
  168.8 3.1 fusion.18
  171.9 3.1 fusion.17
  175.3 1.1 dynamic-slice_bitcast_fusion.5
  176.4 1.0 collective-permute-start.6
  177.4 2.2 collective-permute-start.5
  179.6 3.1 fusion.23
  182.7 3.1 fusion.22
  185.8 3.1 fusion.21
  188.9 2.7 fusion.20
  191.8 1.2 copy-done.2
  193.0 1.0 dynamic-slice_bitcast_fusion.2
  194.8 2.1 collective-permute-start.11
  197.7 1.9 collective-permute-start.10
  199.5 15.3 %collective-permute-done.12 = bf16[320,640]{1,0:T(8,128)(2,1)S(1)} collective-permute-done((bf16[320,640]{1,0:T(8,128)(2,1)}, bf16[320,640]{1,0:T(8,128)(2,1)S(1)}, u32[]{:S(2)}, u32[]{:S(2)}) %collective-permute-start.12) | collective-permute-done | bytes 409632 | tf_op jit(solution)/shard_map/ppermute | solution.py:30
  215.8 2.1 broadcast_select_fusion.2
  218.0 1.1 fusion.45
  219.1 1.6 collective-permute-start.16
  220.7 1.6 collective-permute-start.15
  222.3 2.4 collective-permute-start.14
  224.7 5.5 %collective-permute-start.13 = (bf16[160,640]{1,0:T(8,128)(2,1)S(1)}, bf16[160,640]{1,0:T(8,128)(2,1)}, u32[]{:S(2)}, u32[]{:S(2)}) collective-permute-start(bf16[160,640]{1,0:T(8,128)(2,1)S(1)} %get-tuple-element.32), channel_id=1, source_target_pairs={{0,0},{1,32},{2,2},{3,34},{4,4},{5,36},{6,6},{7,38},{8,8},{9,40},{... | collective-permute-start | bytes 614408 | tf_op jit(solution)/shard_map/ppermute | solution.py:30
  230.3 11.1 %collective-permute-done.16 = bf16[160,640]{1,0:T(8,128)(2,1)S(1)} collective-permute-done((bf16[160,640]{1,0:T(8,128)(2,1)}, bf16[160,640]{1,0:T(8,128)(2,1)S(1)}, u32[]{:S(2)}, u32[]{:S(2)}) %collective-permute-start.16) | collective-permute-done | bytes 204832 | tf_op jit(solution)/shard_map/ppermute | solution.py:30
  241.4 5.8 %collective-permute-done.14 = bf16[160,640]{1,0:T(8,128)(2,1)} collective-permute-done((bf16[160,640]{1,0:T(8,128)(2,1)}, bf16[160,640]{1,0:T(8,128)(2,1)}, u32[]{:S(2)}, u32[]{:S(2)}) %collective-permute-start.14) | collective-permute-done | bytes 204832 | tf_op jit(solution)/shard_map/ppermute | solution.py:30
  247.2 1.3 collective-permute-done.13
  248.5 2.4 subtract_convert_fusion
  251.6 2.7 convolution_convert_fusion
  254.8 1.4 constant_dynamic-slice_fusion.9
  256.3 3.3 %collective-permute-start.19 = (bf16[512,160]{0,1:T(8,128)(2,1)S(1)}, bf16[512,160]{0,1:T(8,128)(2,1)S(1)}, u32[]{:S(2)}, u32[]{:S(2)}) collective-permute-start(bf16[512,160]{0,1:T(8,128)(2,1)S(1)} %bitcast.178), channel_id=1, source_target_pairs={{0,128},{1,129},{2,192},{3,193},{4,0},{5,1},{6,64},{7,65},{8,136},... | collective-permute-start | bytes 491528 | tf_op jit(solution)/shard_map/ppermute | solution.py:30
  259.6 1.9 collective-permute-start.18
  261.5 4.3 %collective-permute-start.17 = (bf16[512,160]{0,1:T(8,128)(2,1)S(1)}, bf16[512,160]{0,1:T(8,128)(2,1)S(1)}, u32[]{:S(2)}, u32[]{:S(2)}) collective-permute-start(bf16[512,160]{0,1:T(8,128)(2,1)S(1)} %bitcast.180), channel_id=1, source_target_pairs={{0,0},{1,1},{2,64},{3,65},{4,128},{5,129},{6,192},{7,193},{8,8},{9... | collective-permute-start | bytes 491528 | tf_op jit(solution)/shard_map/ppermute | solution.py:30
  266.1 2.6 collective-permute-done.19
  268.7 1.2 collective-permute-done.18
  269.8 6.0 %collective-permute-done.17 = bf16[512,160]{0,1:T(8,128)(2,1)S(1)} collective-permute-done((bf16[512,160]{0,1:T(8,128)(2,1)S(1)}, bf16[512,160]{0,1:T(8,128)(2,1)S(1)}, u32[]{:S(2)}, u32[]{:S(2)}) %collective-permute-start.17) | collective-permute-done | bytes 163872 | tf_op jit(solution)/shard_map/ppermute | solution.py:30
  276.6 9.7 %collective-permute-done.21 = f32[256,160]{0,1:T(8,128)S(1)} collective-permute-done((f32[256,160]{0,1:T(8,128)S(1)}, f32[256,160]{0,1:T(8,128)S(1)}, u32[]{:S(2)}, u32[]{:S(2)}) %collective-permute-start.21) | collective-permute-done | bytes 163872 | tf_op jit(solution)/shard_map/ppermute | solution.py:30
  287.5 7.9 %collective-permute-start.23 = (f32[64,160]{1,0:T(8,128)S(1)}, f32[64,160]{1,0:T(8,128)S(1)}, u32[]{:S(2)}, u32[]{:S(2)}) collective-permute-start(f32[64,160]{1,0:T(8,128)S(1)} %get-tuple-element.49), channel_id=1, source_target_pairs={{0,8},{1,40},{2,10},{3,42},{4,12},{5,44},{6,14},{7,46},{8,0},{9,32... | collective-permute-start | bytes 122888 | tf_op jit(solution)/shard_map/ppermute | solution.py:30
  295.4 1.9 collective-permute-start.22
  298.1 5.6 %collective-permute-done.22 = f32[64,160]{1,0:T(8,128)S(1)} collective-permute-done((f32[64,160]{1,0:T(8,128)S(1)}, f32[64,160]{1,0:T(8,128)S(1)}, u32[]{:S(2)}, u32[]{:S(2)}) %collective-permute-start.22) | collective-permute-done | bytes 40992 | tf_op jit(solution)/shard_map/ppermute | solution.py:30
  (107 shorter events, 13.7 us)
Async XLA Ops:
  7.2 8.9 %copy-start = (bf16[16,1,512,128]{3,2,1,0:T(8,128)(2,1)S(1)}, bf16[16,1,512,128]{3,2,1,0:T(8,128)(2,1)}, u32[]{:S(2)}) copy-start(bf16[16,1,512,128]{3,2,1,0:T(8,128)(2,1)} %param.25) | copy-start | bytes 6291460
  7.2 243.7 %all-gather.2.cloned.1.call-start = ((), (), s32[]{:S(2)}) async-start(), calls=%async_computation | async-start | bytes 2703360 | tf_op jit(solution)/shard_map/all_gather | solution.py:143
  7.2 105.9 %collective-permute-start.8 = (bf16[1024,640]{1,0:T(8,128)(2,1)}, bf16[1024,640]{1,0:T(8,128)(2,1)}, u32[]{:S(2)}, u32[]{:S(2)}) collective-permute-start(bf16[1024,640]{1,0:T(8,128)(2,1)} %param.15), channel_id=1, source_target_pairs={{0,1},{1,0},{2,3},{3,2},{4,5},{5,4},{6,7},{7,6},{8,9},{9,8},{10,11... | collective-permute-start | bytes 3932168 | tf_op jit(solution)/shard_map/ppermute | solution.py:30
  11.8 101.6 %collective-permute-start.1 = (bf16[1024,640]{1,0:T(8,128)(2,1)}, bf16[1024,640]{1,0:T(8,128)(2,1)}, u32[]{:S(2)}, u32[]{:S(2)}) collective-permute-start(bf16[1024,640]{1,0:T(8,128)(2,1)} %param.15), channel_id=1, source_target_pairs={{0,8},{1,9},{2,10},{3,11},{4,12},{5,13},{6,14},{7,15},{8,0},{9,1},... | collective-permute-start | bytes 3932168 | tf_op jit(solution)/shard_map/ppermute | solution.py:30
  11.8 3.4 %copy-start.8 = (bf16[16,4,640]{2,1,0:T(4,128)(2,1)S(1)}, bf16[16,4,640]{2,1,0:T(4,128)(2,1)}, u32[]{:S(2)}) copy-start(bf16[16,4,640]{2,1,0:T(4,128)(2,1)} %param.22) | copy-start | bytes 245764
  11.8 3.4 %copy-start.9 = (s32[16]{0:T(128)S(1)}, s32[16]{0:T(128)}, u32[]{:S(2)}) copy-start(s32[16]{0:T(128)} %param.27) | copy-start | bytes 196
  11.8 3.5 %copy-start.13 = (bf16[16,4,128]{2,1,0:T(4,128)(2,1)S(1)}, bf16[16,4,128]{2,1,0:T(4,128)(2,1)}, u32[]{:S(2)}) copy-start(bf16[16,4,128]{2,1,0:T(4,128)(2,1)} %param.23) | copy-start | bytes 49156
  14.7 91.1 %collective-permute-start = (bf16[1024,320]{0,1:T(8,128)(2,1)}, bf16[1024,320]{0,1:T(8,128)(2,1)S(1)}, u32[]{:S(2)}, u32[]{:S(2)}) collective-permute-start(bf16[1024,320]{0,1:T(8,128)(2,1)} %bitcast.2), channel_id=1, source_target_pairs={{0,8},{1,9},{2,10},{3,11},{4,12},{5,13},{6,14},{7,15},{8,0},{9,1},... | collective-permute-start | bytes 1966088 | tf_op jit(solution)/shard_map/ppermute | solution.py:30
  15.2 2.2 copy-start.14
  16.0 1.7 copy-start.11
  17.8 1.3 copy-start.10
  17.8 87.7 %copy-start.15 = (s32[64]{0:T(128)S(1)}, s32[64]{0:T(128)}, u32[]{:S(2)}) copy-start(s32[64]{0:T(128)} %param.18) | copy-start | bytes 772
  17.8 88.0 %copy-start.3 = (bf16[1024,2,1,160]{0,3,2,1:T(8,128)(2,1)S(1)}, bf16[1024,2,1,160]{0,3,2,1:T(8,128)(2,1)}, u32[]{:S(2)}) copy-start(bf16[1024,2,1,160]{0,3,2,1:T(8,128)(2,1)} %get-tuple-element.30) | copy-start | bytes 1966084
  107.0 32.6 %collective-permute-start.4 = (bf16[2048,320]{0,1:T(8,128)(2,1)}, bf16[2048,320]{0,1:T(8,128)(2,1)}, u32[]{:S(2)}, u32[]{:S(2)}) collective-permute-start(bf16[2048,320]{0,1:T(8,128)(2,1)} %pad_maximum_fusion.2), channel_id=1, source_target_pairs={{0,2},{1,3},{2,4},{3,5},{4,6},{5,7},{6,0},{7,1},{8,10},{9,11},{10,... | collective-permute-start | bytes 3932168 | tf_op jit(solution)/shard_map/ppermute | solution.py:30
  108.6 60.2 %collective-permute-start.3 = (bf16[2048,320]{0,1:T(8,128)(2,1)}, bf16[2048,320]{0,1:T(8,128)(2,1)}, u32[]{:S(2)}, u32[]{:S(2)}) collective-permute-start(bf16[2048,320]{0,1:T(8,128)(2,1)} %pad_maximum_fusion.2), channel_id=1, source_target_pairs={{0,4},{1,5},{2,6},{3,7},{4,0},{5,1},{6,2},{7,3},{8,12},{9,13},{10,... | collective-permute-start | bytes 3932168 | tf_op jit(solution)/shard_map/ppermute | solution.py:30
  111.7 60.2 %collective-permute-start.2 = (bf16[2048,320]{0,1:T(8,128)(2,1)}, bf16[2048,320]{0,1:T(8,128)(2,1)}, u32[]{:S(2)}, u32[]{:S(2)}) collective-permute-start(bf16[2048,320]{0,1:T(8,128)(2,1)} %pad_maximum_fusion.2), channel_id=1, source_target_pairs={{0,6},{1,7},{2,0},{3,1},{4,2},{5,3},{6,4},{7,5},{8,14},{9,15},{10,... | collective-permute-start | bytes 3932168 | tf_op jit(solution)/shard_map/ppermute | solution.py:30
  113.2 66.5 %collective-permute-start.9 = (bf16[1024,640]{1,0:T(8,128)(2,1)}, bf16[1024,640]{1,0:T(8,128)(2,1)S(1)}, u32[]{:S(2)}, u32[]{:S(2)}) collective-permute-start(bf16[1024,640]{1,0:T(8,128)(2,1)} %collective-permute-done.8), channel_id=1, source_target_pairs={{0,8},{1,9},{2,10},{3,11},{4,12},{5,13},{6,14},{7,15},{8,0},{9,1},... | collective-permute-start | bytes 3932168 | tf_op jit(solution)/shard_map/ppermute | solution.py:30
  113.4 26.2 %copy-start.12 = (bf16[1024,640]{1,0:T(8,128)(2,1)S(1)}, bf16[1024,640]{1,0:T(8,128)(2,1)}, u32[]{:S(2)}) copy-start(bf16[1024,640]{1,0:T(8,128)(2,1)} %param.15) | copy-start | bytes 3932164
  175.3 7.4 %copy-start.1 = (bf16[4,320,640]{2,1,0:T(8,128)(2,1)}, bf16[4,320,640]{2,1,0:T(8,128)(2,1)S(1)}, u32[]{:S(2)}) copy-start(bf16[4,320,640]{2,1,0:T(8,128)(2,1)S(1)} %pad_maximum_fusion) | copy-start | bytes 4915204
  176.4 21.3 %collective-permute-start.7 = (bf16[320,640]{1,0:T(8,128)(2,1)S(1)}, bf16[320,640]{1,0:T(8,128)(2,1)}, u32[]{:S(2)}, u32[]{:S(2)}) collective-permute-start(bf16[320,640]{1,0:T(8,128)(2,1)S(1)} %get-tuple-element.25), channel_id=1, source_target_pairs={{0,192},{1,193},{2,194},{3,195},{4,196},{5,197},{6,198},{7,199},{8... | collective-permute-start | bytes 1228808 | tf_op jit(solution)/shard_map/ppermute | solution.py:30
  176.4 23.1 %collective-permute-start.6 = (bf16[320,640]{1,0:T(8,128)(2,1)}, bf16[320,640]{1,0:T(8,128)(2,1)}, u32[]{:S(2)}, u32[]{:S(2)}) collective-permute-start(bf16[320,640]{1,0:T(8,128)(2,1)} %get-tuple-element.26), channel_id=1, source_target_pairs={{0,128},{1,129},{2,130},{3,131},{4,132},{5,133},{6,134},{7,135},{8... | collective-permute-start | bytes 1228808 | tf_op jit(solution)/shard_map/ppermute | solution.py:30
  177.4 22.1 %collective-permute-start.5 = (bf16[320,640]{1,0:T(8,128)(2,1)}, bf16[320,640]{1,0:T(8,128)(2,1)}, u32[]{:S(2)}, u32[]{:S(2)}) collective-permute-start(bf16[320,640]{1,0:T(8,128)(2,1)} %get-tuple-element.24), channel_id=1, source_target_pairs={{0,64},{1,65},{2,66},{3,67},{4,68},{5,69},{6,70},{7,71},{8,72},{9,... | collective-permute-start | bytes 1228808 | tf_op jit(solution)/shard_map/ppermute | solution.py:30
  191.8 1.2 copy-start.2
  194.0 20.9 %collective-permute-start.12 = (bf16[320,640]{1,0:T(8,128)(2,1)}, bf16[320,640]{1,0:T(8,128)(2,1)S(1)}, u32[]{:S(2)}, u32[]{:S(2)}) collective-permute-start(bf16[320,640]{1,0:T(8,128)(2,1)} %get-tuple-element.28), channel_id=1, source_target_pairs={{0,192},{1,193},{2,194},{3,195},{4,196},{5,197},{6,198},{7,199},{8... | collective-permute-start | bytes 1228808 | tf_op jit(solution)/shard_map/ppermute | solution.py:30
  194.8 20.0 %collective-permute-start.11 = (bf16[320,640]{1,0:T(8,128)(2,1)}, bf16[320,640]{1,0:T(8,128)(2,1)S(1)}, u32[]{:S(2)}, u32[]{:S(2)}) collective-permute-start(bf16[320,640]{1,0:T(8,128)(2,1)} %get-tuple-element.29), channel_id=1, source_target_pairs={{0,128},{1,129},{2,130},{3,131},{4,132},{5,133},{6,134},{7,135},{8... | collective-permute-start | bytes 1228808 | tf_op jit(solution)/shard_map/ppermute | solution.py:30
  197.7 18.2 %collective-permute-start.10 = (bf16[320,640]{1,0:T(8,128)(2,1)S(1)}, bf16[320,640]{1,0:T(8,128)(2,1)}, u32[]{:S(2)}, u32[]{:S(2)}) collective-permute-start(bf16[320,640]{1,0:T(8,128)(2,1)S(1)} %get-tuple-element.27), channel_id=1, source_target_pairs={{0,64},{1,65},{2,66},{3,67},{4,68},{5,69},{6,70},{7,71},{8,72},{9,... | collective-permute-start | bytes 1228808 | tf_op jit(solution)/shard_map/ppermute | solution.py:30
  199.5 48.9 %copy-start.7 = (bf16[160,640]{1,0:T(8,128)(2,1)S(1)}, bf16[160,640]{1,0:T(8,128)(2,1)}, u32[]{:S(2)}) copy-start(bf16[160,640]{1,0:T(8,128)(2,1)} %param.19) | copy-start | bytes 614404
  215.8 32.6 %copy-start.5 = (f32[160,640]{1,0:T(8,128)S(1)}, f32[160,640]{1,0:T(8,128)}, u32[]{:S(2)}) copy-start(f32[160,640]{1,0:T(8,128)} %param.20) | copy-start | bytes 1228804
  218.0 30.5 %copy-start.6 = (f32[160,640]{1,0:T(8,128)S(1)}, f32[160,640]{1,0:T(8,128)}, u32[]{:S(2)}) copy-start(f32[160,640]{1,0:T(8,128)} %param.21) | copy-start | bytes 1228804
  219.1 22.3 %collective-permute-start.16 = (bf16[160,640]{1,0:T(8,128)(2,1)}, bf16[160,640]{1,0:T(8,128)(2,1)S(1)}, u32[]{:S(2)}, u32[]{:S(2)}) collective-permute-start(bf16[160,640]{1,0:T(8,128)(2,1)} %get-tuple-element.35), channel_id=1, source_target_pairs={{0,17},{1,49},{2,19},{3,51},{4,21},{5,53},{6,23},{7,55},{8,25},{9,... | collective-permute-start | bytes 614408 | tf_op jit(solution)/shard_map/ppermute | solution.py:30
  220.7 20.7 %collective-permute-start.15 = (bf16[160,640]{1,0:T(8,128)(2,1)}, bf16[160,640]{1,0:T(8,128)(2,1)}, u32[]{:S(2)}, u32[]{:S(2)}) collective-permute-start(bf16[160,640]{1,0:T(8,128)(2,1)} %get-tuple-element.34), channel_id=1, source_target_pairs={{0,1},{1,33},{2,3},{3,35},{4,5},{5,37},{6,7},{7,39},{8,9},{9,41},{... | collective-permute-start | bytes 614408 | tf_op jit(solution)/shard_map/ppermute | solution.py:30
  222.3 24.9 %collective-permute-start.14 = (bf16[160,640]{1,0:T(8,128)(2,1)}, bf16[160,640]{1,0:T(8,128)(2,1)}, u32[]{:S(2)}, u32[]{:S(2)}) collective-permute-start(bf16[160,640]{1,0:T(8,128)(2,1)} %get-tuple-element.33), channel_id=1, source_target_pairs={{0,16},{1,48},{2,18},{3,50},{4,20},{5,52},{6,22},{7,54},{8,24},{9,... | collective-permute-start | bytes 614408 | tf_op jit(solution)/shard_map/ppermute | solution.py:30
  224.7 23.7 %collective-permute-start.13 = (bf16[160,640]{1,0:T(8,128)(2,1)S(1)}, bf16[160,640]{1,0:T(8,128)(2,1)}, u32[]{:S(2)}, u32[]{:S(2)}) collective-permute-start(bf16[160,640]{1,0:T(8,128)(2,1)S(1)} %get-tuple-element.32), channel_id=1, source_target_pairs={{0,0},{1,32},{2,2},{3,34},{4,4},{5,36},{6,6},{7,38},{8,8},{9,40},{... | collective-permute-start | bytes 614408 | tf_op jit(solution)/shard_map/ppermute | solution.py:30
  250.9 0.7 copy-start.4
  256.2 9.9 %collective-permute-start.20 = (bf16[512,160]{0,1:T(8,128)(2,1)S(1)}, bf16[512,160]{0,1:T(8,128)(2,1)S(1)}, u32[]{:S(2)}, u32[]{:S(2)}) collective-permute-start(bf16[512,160]{0,1:T(8,128)(2,1)S(1)} %bitcast.177), channel_id=1, source_target_pairs={{0,192},{1,193},{2,128},{3,129},{4,64},{5,65},{6,0},{7,1},{8,200},... | collective-permute-start | bytes 491528 | tf_op jit(solution)/shard_map/ppermute | solution.py:30
  256.3 12.4 %collective-permute-start.19 = (bf16[512,160]{0,1:T(8,128)(2,1)S(1)}, bf16[512,160]{0,1:T(8,128)(2,1)S(1)}, u32[]{:S(2)}, u32[]{:S(2)}) collective-permute-start(bf16[512,160]{0,1:T(8,128)(2,1)S(1)} %bitcast.178), channel_id=1, source_target_pairs={{0,128},{1,129},{2,192},{3,193},{4,0},{5,1},{6,64},{7,65},{8,136},... | collective-permute-start | bytes 491528 | tf_op jit(solution)/shard_map/ppermute | solution.py:30
  259.6 10.2 %collective-permute-start.18 = (bf16[512,160]{0,1:T(8,128)(2,1)S(1)}, bf16[512,160]{0,1:T(8,128)(2,1)S(1)}, u32[]{:S(2)}, u32[]{:S(2)}) collective-permute-start(bf16[512,160]{0,1:T(8,128)(2,1)S(1)} %bitcast.179), channel_id=1, source_target_pairs={{0,64},{1,65},{2,0},{3,1},{4,192},{5,193},{6,128},{7,129},{8,72},{... | collective-permute-start | bytes 491528 | tf_op jit(solution)/shard_map/ppermute | solution.py:30
  261.5 14.3 %collective-permute-start.17 = (bf16[512,160]{0,1:T(8,128)(2,1)S(1)}, bf16[512,160]{0,1:T(8,128)(2,1)S(1)}, u32[]{:S(2)}, u32[]{:S(2)}) collective-permute-start(bf16[512,160]{0,1:T(8,128)(2,1)S(1)} %bitcast.180), channel_id=1, source_target_pairs={{0,0},{1,1},{2,64},{3,65},{4,128},{5,129},{6,192},{7,193},{8,8},{9... | collective-permute-start | bytes 491528 | tf_op jit(solution)/shard_map/ppermute | solution.py:30
  276.4 9.9 %collective-permute-start.21 = (f32[256,160]{0,1:T(8,128)S(1)}, f32[256,160]{0,1:T(8,128)S(1)}, u32[]{:S(2)}, u32[]{:S(2)}) collective-permute-start(f32[256,160]{0,1:T(8,128)S(1)} %bitcast.176), channel_id=1, source_target_pairs={{0,1},{1,0},{2,3},{3,2},{4,5},{5,4},{6,7},{7,6},{8,9},{9,8},{10,11... | collective-permute-start | bytes 491528 | tf_op jit(solution)/shard_map/ppermute | solution.py:30
  286.5 10.8 %collective-permute-start.25 = (f32[64,160]{1,0:T(8,128)S(1)}, f32[64,160]{1,0:T(8,128)S(1)}, u32[]{:S(2)}, u32[]{:S(2)}) collective-permute-start(f32[64,160]{1,0:T(8,128)S(1)} %get-tuple-element.47), channel_id=1, source_target_pairs={{0,24},{1,56},{2,26},{3,58},{4,28},{5,60},{6,30},{7,62},{8,16},{9,... | collective-permute-start | bytes 122888 | tf_op jit(solution)/shard_map/ppermute | solution.py:30
  286.6 10.7 %collective-permute-start.24 = (f32[64,160]{1,0:T(8,128)S(1)}, f32[64,160]{1,0:T(8,128)S(1)}, u32[]{:S(2)}, u32[]{:S(2)}) collective-permute-start(f32[64,160]{1,0:T(8,128)S(1)} %get-tuple-element.48), channel_id=1, source_target_pairs={{0,16},{1,48},{2,18},{3,50},{4,20},{5,52},{6,22},{7,54},{8,24},{9,... | collective-permute-start | bytes 122888 | tf_op jit(solution)/shard_map/ppermute | solution.py:30
  287.5 10.5 %collective-permute-start.23 = (f32[64,160]{1,0:T(8,128)S(1)}, f32[64,160]{1,0:T(8,128)S(1)}, u32[]{:S(2)}, u32[]{:S(2)}) collective-permute-start(f32[64,160]{1,0:T(8,128)S(1)} %get-tuple-element.49), channel_id=1, source_target_pairs={{0,8},{1,40},{2,10},{3,42},{4,12},{5,44},{6,14},{7,46},{8,0},{9,32... | collective-permute-start | bytes 122888 | tf_op jit(solution)/shard_map/ppermute | solution.py:30
  295.4 8.3 %collective-permute-start.22 = (f32[64,160]{1,0:T(8,128)S(1)}, f32[64,160]{1,0:T(8,128)S(1)}, u32[]{:S(2)}, u32[]{:S(2)}) collective-permute-start(f32[64,160]{1,0:T(8,128)S(1)} %get-tuple-element.46), channel_id=1, source_target_pairs={{0,0},{1,32},{2,2},{3,34},{4,4},{5,36},{6,6},{7,38},{8,8},{9,40},{... | collective-permute-start | bytes 122888 | tf_op jit(solution)/shard_map/ppermute | solution.py:30
Sparse Core Ops, SparseCore 0:
  19.2 94.2 all-gather.1
